TPU v7x, 32 devices: a whole 2x2x4 slice. The times are simulated.
32 devices in a mesh: depth: 4 (over y, core), az: 8 (over z, x).
Axes of the slice: x: 2, y: 2, z: 4, core: 2. Of those that a mesh axis runs over, the one named last changes fastest.
Arguments:
- pressure_field: float32 [2, 2048, 4096], P(None, 'depth', 'az'), may hold values from -6 to 6
- block_inverses: float32 [2, 8, 16, 128, 128], P(None, None, 'depth'), may hold values from -1.25 to 1.25, as said below
- lower_spikes: float32 [2, 8, 16, 128], P(None, None, 'depth'), may hold values from -1 to 1, as said below
- upper_spikes: float32 [2, 8, 16, 128], P(None, None, 'depth'), may hold values from -1 to 1, as said below
- pade_weights: float32 [2, 8], replicated, may hold values from -0.08 to 0.08
- layer_wavenumber: float32 [2, 5], replicated, may hold values from -0.4 to 0.4
- layer_index: int32 [16], P('depth'), may hold values from 0 to 4
- depth_coupling: float32 [2048], P('depth'), may hold values from 0.05 to 1
- attenuation: float32 [5, 6], replicated, may hold values from 0.02 to 0.4
- sediment_type: int32 [4096], P('az'), may hold values from 0 to 5
Outputs:
- final_field: float32 [2, 2048, 4096], P(None, 'depth', 'az')
Inputs may be any that keep to these rules, and one draw needn't show every extreme that they name: `block_inverses`: complex blocks whose diagonal entries have real parts between 0.75 and 1.25, every other entry smaller in magnitude than the diagonal ones. `lower_spikes`: the last entry of each spike has magnitude below 1. `upper_spikes`: the first entry of each spike has magnitude below 1.
All inputs are finite; a program needn't handle non-finite values.
Results may differ from a plain program's by a relative error of at most 0.0001.
Values sent between devices are 32-bit elements; how exact they have to be, the bound alone decides.
A program may use at most 128 MiB of HBM per device.

v0:
```python
import math
import jax
import jax.numpy as jnp
from jax import lax
from jax.sharding import PartitionSpec as P

AZ_ROWS = 32
AZ_COLS = 128
STEPS = 2
FULL_PRECISION = lax.Precision.HIGHEST


def entering_2(value, axis, combine, identity, reverse):
    size, index = (lax.axis_size(axis), lax.axis_index(axis))
    everything = jax.tree.map(lambda part: lax.all_gather(part, axis), value)
    start = jax.tree.map(
        lambda part, zero: jnp.broadcast_to(jnp.asarray(zero, part.dtype), part.shape),
        value,
        identity,
    )

    def hop(k, before):
        at = size - 1 - k if reverse else k
        reached = at > index if reverse else at < index
        new = combine(before, jax.tree.map(lambda part: part[at], everything))
        return jax.tree.map(lambda a, b: jnp.where(reached, a, b), new, before)

    return lax.fori_loop(0, size, hop, start)


def extended(cells, sides, width):
    for axis, dim in sides:
        count = lax.axis_size(axis)
        ends = count - 1
        head = lax.slice_in_dim(cells, 0, width, axis=dim)
        tail = lax.slice_in_dim(cells, cells.shape[dim] - width, cells.shape[dim], axis=dim)
        cells = jnp.concatenate(
            [
                lax.ppermute(tail, axis, [(i, (i + 1) % count) for i in range(ends)]),
                cells,
                lax.ppermute(head, axis, [((i + 1) % count, i) for i in range(ends)]),
            ],
            axis=dim,
        )
    return cells


def complex_einsum(formula, left_re, left_im, right_re, right_im):
    real_part = jnp.einsum(formula, left_re, right_re, precision=FULL_PRECISION) - jnp.einsum(
        formula, left_im, right_im, precision=FULL_PRECISION
    )
    imag_part = jnp.einsum(formula, left_re, right_im, precision=FULL_PRECISION) + jnp.einsum(
        formula, left_im, right_re, precision=FULL_PRECISION
    )
    return (real_part, imag_part)


def compose(earlier, later):
    a_re, a_im, b_re, b_im = earlier
    c_re, c_im, d_re, d_im = later
    return (
        c_re * a_re - c_im * a_im,
        c_re * a_im + c_im * a_re,
        c_re[:, None] * b_re - c_im[:, None] * b_im + d_re,
        c_re[:, None] * b_im + c_im[:, None] * b_re + d_im,
    )


def apply_map(factor_re, factor_im, offset_re, offset_im, carried):
    return (
        factor_re[:, None] * carried[0] - factor_im[:, None] * carried[1] + offset_re,
        factor_re[:, None] * carried[1] + factor_im[:, None] * carried[0] + offset_im,
    )


def neutral_map(block_map):
    return (
        jnp.ones_like(block_map[0]),
        jnp.zeros_like(block_map[1]),
        jnp.zeros_like(block_map[2]),
        jnp.zeros_like(block_map[3]),
    )


def block_maps(factor_re, factor_im, offset_re, offset_im, ordering):
    combined = (
        jnp.ones_like(factor_re[:, 0]),
        jnp.zeros_like(factor_im[:, 0]),
        jnp.zeros_like(offset_re[:, 0]),
        jnp.zeros_like(offset_im[:, 0]),
    )
    for block_pos in ordering:
        combined = compose(
            combined,
            (
                factor_re[:, block_pos],
                factor_im[:, block_pos],
                offset_re[:, block_pos],
                offset_im[:, block_pos],
            ),
        )
    return combined


def block_carries(start_value, factor_re, factor_im, offset_re, offset_im, ordering):
    carried = start_value
    entering = [None] * factor_re.shape[1]
    for block_pos in ordering:
        entering[block_pos] = carried
        carried = apply_map(
            factor_re[:, block_pos],
            factor_im[:, block_pos],
            offset_re[:, block_pos],
            offset_im[:, block_pos],
            carried,
        )
    return (
        jnp.stack([entry[0] for entry in entering], axis=1),
        jnp.stack([entry[1] for entry in entering], axis=1),
    )


def link_forward(block_map):
    prefix = entering_2(
        (block_map[0], block_map[1], block_map[2], block_map[3]),
        "depth",
        compose,
        neutral_map(block_map),
        False,
    )
    result_value = (prefix[2], prefix[3])
    return result_value


def link_backward(block_map):
    prefix = entering_2(
        (block_map[0], block_map[1], block_map[2], block_map[3]),
        "depth",
        compose,
        neutral_map(block_map),
        True,
    )
    result_value = (prefix[2], prefix[3])
    return result_value


def advance(field_part, operator_part, block_inverses, lower_spikes, upper_spikes, pade_weights):
    depth_rows = field_part.shape[1]
    az_count = field_part.shape[2]
    block_count = block_inverses.shape[2]
    block_rows = block_inverses.shape[3]
    shaped = operator_part.reshape(2, block_count, block_rows, az_count)
    solved_re, solved_im = complex_einsum(
        "tbij,bjn->tbin", block_inverses[0], block_inverses[1], shaped[0], shaped[1]
    )
    lower_re = lower_spikes[0]
    lower_im = lower_spikes[1]
    upward = list(range(block_count))
    factor_re = -lower_re[:, :, -1]
    factor_im = -lower_im[:, :, -1]
    forward_map = block_maps(factor_re, factor_im, solved_re[:, :, -1], solved_im[:, :, -1], upward)
    enter_re, enter_im = block_carries(
        link_forward(forward_map),
        factor_re,
        factor_im,
        solved_re[:, :, -1],
        solved_im[:, :, -1],
        upward,
    )
    swept_re = solved_re - (
        lower_re[..., None] * enter_re[:, :, None] - lower_im[..., None] * enter_im[:, :, None]
    )
    swept_im = solved_im - (
        lower_re[..., None] * enter_im[:, :, None] + lower_im[..., None] * enter_re[:, :, None]
    )
    upper_re = upper_spikes[0]
    upper_im = upper_spikes[1]
    downward = list(reversed(range(block_count)))
    back_factor_re = -upper_re[:, :, 0]
    back_factor_im = -upper_im[:, :, 0]
    backward_map = block_maps(
        back_factor_re, back_factor_im, swept_re[:, :, 0], swept_im[:, :, 0], downward
    )
    below_re, below_im = block_carries(
        link_backward(backward_map),
        back_factor_re,
        back_factor_im,
        swept_re[:, :, 0],
        swept_im[:, :, 0],
        downward,
    )
    final_re = swept_re - (
        upper_re[..., None] * below_re[:, :, None] - upper_im[..., None] * below_im[:, :, None]
    )
    final_im = swept_im - (
        upper_re[..., None] * below_im[:, :, None] + upper_im[..., None] * below_re[:, :, None]
    )
    incr_re = jnp.einsum(
        "t,tbin->bin", pade_weights[0], final_re, precision=FULL_PRECISION
    ) - jnp.einsum("t,tbin->bin", pade_weights[1], final_im, precision=FULL_PRECISION)
    incr_im = jnp.einsum(
        "t,tbin->bin", pade_weights[0], final_im, precision=FULL_PRECISION
    ) + jnp.einsum("t,tbin->bin", pade_weights[1], final_re, precision=FULL_PRECISION)
    return field_part + jnp.stack([incr_re, incr_im]).reshape(2, depth_rows, az_count)


def dft_table(length, sign_factor):
    product = jnp.arange(length)[:, None] * jnp.arange(length)[None, :] % length
    angles = 2.0 * math.pi / length * product.astype(jnp.float32)
    return (jnp.cos(angles), sign_factor * jnp.sin(angles))


def couple_azimuths(columns, coupling_rows):
    row_count = columns.shape[1]
    total_az = columns.shape[2]
    shaped = columns.reshape(2, row_count, AZ_ROWS, AZ_COLS)
    outer_re, outer_im = dft_table(AZ_ROWS, -1.0)
    inner_re, inner_im = dft_table(AZ_COLS, -1.0)
    twist_index = jnp.arange(AZ_ROWS)[:, None] * jnp.arange(AZ_COLS)[None, :] % total_az
    twist_angle = 2.0 * math.pi / total_az * twist_index.astype(jnp.float32)
    twist_re = jnp.cos(twist_angle)
    twist_im = -jnp.sin(twist_angle)
    section_re, section_im = complex_einsum("ka,cab->ckb", outer_re, outer_im, shaped[0], shaped[1])
    section_re, section_im = (
        section_re * twist_re - section_im * twist_im,
        section_re * twist_im + section_im * twist_re,
    )
    spec_re, spec_im = complex_einsum("ckb,bm->ckm", section_re, section_im, inner_re, inner_im)
    wavenum = jnp.arange(AZ_ROWS)[:, None] + AZ_ROWS * jnp.arange(AZ_COLS)[None, :]
    signed = jnp.where(wavenum < total_az // 2, wavenum, wavenum - total_az).astype(jnp.float32)
    spatial = (2.0 * jnp.pi * signed / total_az) ** 2
    phase_angle = coupling_rows[:, None, None] * spatial[None]
    rot_re = jnp.cos(phase_angle)
    rot_im = -jnp.sin(phase_angle)
    spec_re, spec_im = (spec_re * rot_re - spec_im * rot_im, spec_re * rot_im + spec_im * rot_re)
    back_re, back_im = complex_einsum("ckm,mb->ckb", spec_re, spec_im, inner_re, -inner_im)
    back_re, back_im = (
        back_re * twist_re + back_im * twist_im,
        back_im * twist_re - back_re * twist_im,
    )
    out_re, out_im = complex_einsum("ak,ckb->cab", outer_re, -outer_im, back_re, back_im)
    return jnp.stack([out_re, out_im]).reshape(2, row_count, total_az) / total_az


def local(
    pressure_field,
    block_inverses,
    lower_spikes,
    upper_spikes,
    pade_weights,
    layer_wavenumber,
    layer_index,
    depth_coupling,
    attenuation,
    sediment_type,
):
    block_rows = block_inverses.shape[3]
    layer_onehot = (layer_index[:, None] == jnp.arange(layer_wavenumber.shape[1])[None, :]).astype(
        jnp.float32
    )
    wave_blocks = jnp.dot(layer_onehot, layer_wavenumber.T, precision=FULL_PRECISION)
    wave_rows = jnp.repeat(wave_blocks.T, block_rows, axis=1)
    type_onehot = (jnp.arange(attenuation.shape[1])[:, None] == sediment_type[None, :]).astype(
        jnp.float32
    )
    exponent = jnp.dot(
        jnp.dot(layer_onehot, attenuation, precision=FULL_PRECISION),
        type_onehot,
        precision=FULL_PRECISION,
    )
    damp_rows = jnp.repeat(jnp.exp(-exponent), block_rows, axis=0)
    column_count = pressure_field.shape[1] // lax.axis_size("az")
    coupling_rows = lax.dynamic_slice_in_dim(
        depth_coupling, lax.axis_index("az") * column_count, column_count
    )
    pressure = pressure_field
    for range_step in range(STEPS):
        padded = extended(pressure, (("depth", 1),), 1)
        laplace = padded[:, 2:] + padded[:, :-2] - 2.0 * pressure
        operator_field = jnp.stack(
            [
                laplace[0]
                + wave_rows[0][:, None] * pressure[0]
                - wave_rows[1][:, None] * pressure[1],
                laplace[1]
                + wave_rows[0][:, None] * pressure[1]
                + wave_rows[1][:, None] * pressure[0],
            ]
        )
        columns = lax.all_to_all(
            advance(
                pressure, operator_field, block_inverses, lower_spikes, upper_spikes, pade_weights
            ),
            "az",
            split_axis=1,
            concat_axis=2,
            tiled=True,
        )
        coupled = couple_azimuths(columns, coupling_rows)
        pressure = (
            lax.all_to_all(coupled, "az", split_axis=2, concat_axis=1, tiled=True) * damp_rows[None]
        )
    return pressure


def solution(mesh):
    in_specs = (
        P(None, "depth", "az"),
        P(None, None, "depth", None, None),
        P(None, None, "depth", None),
        P(None, None, "depth", None),
        P(),
        P(),
        P("depth"),
        P("depth"),
        P(),
        P("az"),
    )
    out_specs = P(None, "depth", "az")
    return jax.shard_map(local, mesh=mesh, in_specs=in_specs, out_specs=out_specs, check_vma=False)
```

profile of v0, /device:TPU:0, one launch (start us, length us, event | category | flops | bytes accessed | tf_op | source)
XLA Modules:
  0.0 754.1 jit_solution(16455060894155055137)
XLA Ops:
  49.8 9.6 %fusion.46 = f32[4,512,8,128]{1,2,0,3:T(8,128)} fusion(f32[8,4,128,128]{3,2,1,0:T(8,128)S(1)} %copy-done.22, f32[4,128,512]{2,1,0:T(8,128)S(1)} %get-tuple-element.923), kind=kOutput, calls=%fused_computation.92 | convolution fusion | flops 3221225472 | bytes 11534336 | tf_op jit(solution)/shard_map/tbij,bjn->tbin/dot_general | solution.py:52
  74.1 12.7 %add_bitcast_fusion.1 = f32[8,4,128,512]{3,0,1,2:T(8,128)S(1)} fusion(f32[4,512,8,128]{1,2,0,3:T(8,128)} %fusion.46, f32[8,4,128,128]{3,2,1,0:T(8,128)S(1)} %copy-done.20, f32[4,128,512]{2,1,0:T(8,128)S(1)} %get-tuple-element.924), kind=kOutput, calls=%fused_computation.46 | convolution fusion | flops 3223322624 | bytes 19922944 | tf_op jit(solution)/shard_map/tbij,bjn->tbin/dot_general | solution.py:52
  108.7 14.9 %copy_subtract_fusion.2 = f32[8,4,128,512]{3,2,0,1:T(8,128)} fusion(f32[8,4,128,512]{3,2,0,1:T(8,128)} %copy-done.3, f32[8,4,128,512]{3,0,1,2:T(8,128)} %get-tuple-element.946), kind=kLoop, calls=%fused_computation.37 | loop fusion | flops 2097152 | bytes 25165824 | tf_op jit(solution)/shard_map/sub | solution.py:170
  124.8 18.8 %copy_subtract_fusion.1 = f32[8,4,128,512]{3,2,0,1:T(8,128)} fusion(f32[8,4,128,512]{3,0,1,2:T(8,128)} %get-tuple-element.945, f32[8,4,128,512]{3,0,1,2:T(8,128)} %copy-done.10), kind=kLoop, calls=%fused_computation.36 | loop fusion | flops 2097152 | bytes 25165824 | tf_op jit(solution)/shard_map/sub | solution.py:173
  165.1 23.1 %fusion.16 = (f32[8,4,128,512]{3,2,0,1:T(8,128)}, f32[8,4,128,512]{3,2,0,1:T(8,128)}) fusion(f32[8,4,128,512]{3,2,0,1:T(8,128)} %copy_subtract_fusion.1, f32[8,4,128,512]{3,0,1,2:T(8,128)} %get-tuple-element.957, f32[8,4,128]{2,0,1:T(8,128)S(1)} %copy.192, f32[8,4,512]{2,0,1:T(8,128)S(1)} %pad_maximum_fusion.7, f32[8,4,128,512]{3,2,0,1:T(8,128)} %copy_subtract_fusion.2, ...), kind=kLoop, calls=%fused_computation.33 | loop fusion | flops 12582912 | bytes 50429952 | tf_op jit(solution)/shard_map/sub | solution.py:195
  188.2 15.2 %fusion.28 = f32[1,4,128,512]{3,0,2,1:T(1,128)S(1)} fusion(f32[8,4,128,512]{3,2,0,1:T(8,128)} %get-tuple-element.955, f32[2,8]{1,0:T(2,128)S(1)} %copy-done.24), kind=kOutput, calls=%fused_computation.58 | convolution fusion | flops 25165824 | bytes 9437696 | tf_op jit(solution)/shard_map/t,tbin->bin/dot_general | solution.py:200
  203.5 10.7 %fusion.26 = f32[1,4,128,512]{3,0,2,1:T(1,128)S(1)} fusion(f32[8,4,128,512]{3,2,0,1:T(8,128)S(1)} %copy-done.2, f32[2,8]{1,0:T(2,128)S(1)} %copy-done.24), kind=kOutput, calls=%fused_computation.56 | convolution fusion | flops 25165824 | bytes 9437696 | tf_op jit(solution)/shard_map/t,tbin->bin/dot_general | solution.py:201
  214.2 10.4 %fusion.32 = f32[1,4,128,512]{3,0,2,1:T(1,128)S(1)} fusion(f32[8,4,128,512]{3,2,0,1:T(8,128)S(1)} %bitcast.805, f32[2,8]{1,0:T(2,128)S(1)} %copy-done.24), kind=kOutput, calls=%fused_computation.62 | convolution fusion | flops 25165824 | bytes 9437696 | tf_op jit(solution)/shard_map/t,tbin->bin/dot_general | solution.py:198
  224.6 10.9 %fusion.30 = f32[1,4,128,512]{3,0,2,1:T(1,128)S(1)} fusion(f32[8,4,128,512]{3,2,0,1:T(8,128)S(1)} %bitcast.805, f32[2,8]{1,0:T(2,128)S(1)} %copy-done.24), kind=kOutput, calls=%fused_computation.60 | convolution fusion | flops 25165824 | bytes 9437696 | tf_op jit(solution)/shard_map/t,tbin->bin/dot_general | solution.py:203
  246.4 47.7 %all-to-all-done = f32[2,512,512]{2,0,1:T(2,128)S(1)} async-done(((f32[2,512,512]{2,0,1:T(2,128)}), f32[2,512,512]{2,0,1:T(2,128)S(1)}, u32[]{:S(2)}, u32[]{:S(2)}) %all-to-all-start) | async-done | bytes 2097184 | tf_op jit(solution)/shard_map/all_to_all | solution.py:290
  345.0 7.5 fusion.397
  352.5 8.1 %reshape.3793 = f32[8,1,65536]{2,1,0:T(1,128)} reshape(f32[4096,2,64]{2,1,0:T(2,128)} %fusion.397) | data formatting | bytes 4194304
  364.7 48.1 %all-to-all-done.1 = f32[8,1,65536]{2,1,0:T(1,128)S(1)} async-done(((f32[8,1,65536]{2,1,0:T(1,128)}), f32[8,1,65536]{2,1,0:T(1,128)S(1)}, u32[]{:S(2)}, u32[]{:S(2)}) %all-to-all-start.1) | async-done | bytes 2097184 | tf_op jit(solution)/shard_map/all_to_all | solution.py:301
  414.6 7.4 reduce
  440.2 7.7 %fusion.44 = f32[4,512,8,128]{1,2,0,3:T(8,128)S(1)} fusion(f32[8,4,128,128]{3,2,1,0:T(8,128)S(1)} %copy-done.23, f32[4,128,512]{2,1,0:T(8,128)S(1)} %get-tuple-element.922), kind=kOutput, calls=%fused_computation.90 | convolution fusion | flops 3221225472 | bytes 11534336 | tf_op jit(solution)/shard_map/tbij,bjn->tbin/dot_general | solution.py:49
  447.9 9.5 %fusion.42 = f32[4,512,8,128]{1,2,0,3:T(8,128)} fusion(f32[8,4,128,128]{3,2,1,0:T(8,128)S(1)} %copy-done.23, f32[4,128,512]{2,1,0:T(8,128)S(1)} %get-tuple-element.921), kind=kOutput, calls=%fused_computation.88 | convolution fusion | flops 3221225472 | bytes 11534336 | tf_op jit(solution)/shard_map/tbij,bjn->tbin/dot_general | solution.py:52
  457.4 7.7 %subtract_bitcast_fusion = f32[8,4,128,512]{3,0,1,2:T(8,128)S(1)} fusion(f32[4,512,8,128]{1,2,0,3:T(8,128)S(1)} %fusion.44, f32[8,4,128,128]{3,2,1,0:T(8,128)S(1)} %copy-done.21, f32[4,128,512]{2,1,0:T(8,128)S(1)} %get-tuple-element.921), kind=kOutput, calls=%fused_computation.43 | convolution fusion | flops 3223322624 | bytes 19922944 | tf_op jit(solution)/shard_map/tbij,bjn->tbin/dot_general | solution.py:49
  465.2 12.8 %add_bitcast_fusion = f32[8,4,128,512]{3,0,1,2:T(8,128)S(1)} fusion(f32[4,512,8,128]{1,2,0,3:T(8,128)} %fusion.42, f32[8,4,128,128]{3,2,1,0:T(8,128)S(1)} %copy-done.21, f32[4,128,512]{2,1,0:T(8,128)S(1)} %get-tuple-element.922), kind=kOutput, calls=%fused_computation.42 | convolution fusion | flops 3223322624 | bytes 19922944 | tf_op jit(solution)/shard_map/tbij,bjn->tbin/dot_general | solution.py:52
  524.8 7.4 add_subtract_fusion
  546.9 7.8 %fusion.24 = f32[1,4,128,512]{3,0,2,1:T(1,128)S(1)} fusion(f32[8,4,128,512]{3,0,1,2:T(8,128)S(1)} %get-tuple-element.942, f32[2,8]{1,0:T(2,128)S(1)} %copy-done.24), kind=kOutput, calls=%fused_computation.54 | convolution fusion | flops 25165824 | bytes 9437696 | tf_op jit(solution)/shard_map/t,tbin->bin/dot_general | solution.py:198
  564.7 52.3 %all_to_all.66 = f32[2,512,512]{2,0,1:T(2,128)S(1)} all-to-all(f32[2,512,512]{2,0,1:T(2,128)S(1)} %copy.141), channel_id=1, replica_groups=mesh['depth'=4,'az'=8] {'az'}, dimensions={1} | all-to-all | bytes 4194304 | tf_op jit(solution)/shard_map/all_to_all | solution.py:290
  667.8 7.5 fusion.396
  682.5 51.9 %all_to_all.67 = f32[8,1,65536]{2,1,0:T(1,128)} all-to-all(f32[8,1,65536]{2,1,0:T(1,128)S(1)} %reshape.3795), channel_id=1, replica_groups=mesh['depth'=4,'az'=8] {'az'}, dimensions={0} | all-to-all | bytes 4194304 | tf_op jit(solution)/shard_map/all_to_all | solution.py:301
  734.3 7.5 reduce.1
  (349 shorter events, 342.0 us)
Async XLA Ops:
  0.0 364.4 %copy-start = (f32[5,6]{1,0:T(8,128)S(1)}, f32[5,6]{1,0:T(8,128)}, u32[]{:S(2)}) copy-start(f32[5,6]{1,0:T(8,128)} %param.26) | copy-start | bytes 364
  1.4 46.2 %collective-permute-start = (f32[2,1,512]{2,1,0:T(1,128)}, f32[2,1,512]{2,1,0:T(1,128)}, u32[]{:S(2)}, u32[]{:S(2)}) collective-permute-start(f32[2,1,512]{2,1,0:T(1,128)} %get-tuple-element.939), channel_id=1, source_target_pairs={{8,0},{16,8},{24,16},{9,1},{17,9},{25,17},{10,2},{18,10},{26,18},{... | collective-permute-start | bytes 12296 | tf_op jit(solution)/shard_map/ppermute | solution.py:41
  2.7 44.9 %copy-start.6 = (f32[2,512,512]{2,1,0:T(8,128)S(1)}, f32[2,512,512]{2,1,0:T(8,128)}, u32[]{:S(2)}) copy-start(f32[2,512,512]{2,1,0:T(8,128)} %param.18) | copy-start | bytes 6291460
  2.7 44.9 %collective-permute-start.1 = (f32[2,1,512]{2,1,0:T(1,128)}, f32[2,1,512]{2,1,0:T(1,128)}, u32[]{:S(2)}, u32[]{:S(2)}) collective-permute-start(f32[2,1,512]{2,1,0:T(1,128)} %get-tuple-element.940), channel_id=1, source_target_pairs={{0,8},{8,16},{16,24},{1,9},{9,17},{17,25},{2,10},{10,18},{18,26},{... | collective-permute-start | bytes 12296 | tf_op jit(solution)/shard_map/ppermute | solution.py:39
  12.1 89.4 %copy-start.27 = (f32[8]{0:T(128)}, f32[8]{0:T(128)S(1)}, u32[]{:S(2)}) copy-start(f32[8]{0:T(128)S(1)} %get-tuple-element.982) | copy-start | bytes 100
  16.6 142.0 %copy-start.25 = (f32[8]{0:T(128)}, f32[8]{0:T(128)S(1)}, u32[]{:S(2)}) copy-start(f32[8]{0:T(128)S(1)} %get-tuple-element.979) | copy-start | bytes 100
  74.1 26.9 %copy-start.30 = (f32[4,1,8]{2,1,0:T(1,128)S(1)}, f32[4,1,8]{2,1,0:T(1,128)}, u32[]{:S(2)}) copy-start(f32[4,1,8]{2,1,0:T(1,128)} %all-gather) | copy-start | bytes 388
  74.1 26.9 %copy-start.31 = (f32[4,1,8]{2,1,0:T(1,128)S(1)}, f32[4,1,8]{2,1,0:T(1,128)}, u32[]{:S(2)}) copy-start(f32[4,1,8]{2,1,0:T(1,128)} %all-gather.1) | copy-start | bytes 388
  74.1 27.3 %copy-start.52 = (f32[8]{0:T(128)S(1)}, f32[8]{0:T(128)}, u32[]{:S(2)}) copy-start(f32[8]{0:T(128)} %get-tuple-element.981) | copy-start | bytes 100
  74.1 27.3 %copy-start.54 = (f32[8]{0:T(128)S(1)}, f32[8]{0:T(128)}, u32[]{:S(2)}) copy-start(f32[8]{0:T(128)} %get-tuple-element.985) | copy-start | bytes 100
  74.1 27.5 %copy-start.17 = (f32[1,8,4,128]{1,2,3,0:T(4,128)S(1)}, f32[1,8,4,128]{1,2,3,0:T(4,128)}, u32[]{:S(2)}) copy-start(f32[1,8,4,128]{1,2,3,0:T(4,128)} %copy.184) | copy-start | bytes 49156
  124.7 20.0 %copy-start.34 = (f32[8]{0:T(128)S(1)}, f32[8]{0:T(128)}, u32[]{:S(2)}) copy-start(f32[8]{0:T(128)} %get-tuple-element.974) | copy-start | bytes 100
  124.7 33.7 %copy-start.50 = (f32[8]{0:T(128)S(1)}, f32[8]{0:T(128)}, u32[]{:S(2)}) copy-start(f32[8]{0:T(128)} %get-tuple-element.973) | copy-start | bytes 100
  124.7 33.7 %copy-start.51 = (f32[8]{0:T(128)S(1)}, f32[8]{0:T(128)}, u32[]{:S(2)}) copy-start(f32[8]{0:T(128)} %get-tuple-element.977) | copy-start | bytes 100
  124.8 33.9 %copy-start.18 = (f32[1,8,4,128]{1,2,3,0:T(4,128)S(1)}, f32[1,8,4,128]{1,2,3,0:T(4,128)}, u32[]{:S(2)}) copy-start(f32[1,8,4,128]{1,2,3,0:T(4,128)} %copy.186) | copy-start | bytes 49156
  124.8 33.9 %copy-start.19 = (f32[1,8,4,128]{1,2,3,0:T(4,128)S(1)}, f32[1,8,4,128]{1,2,3,0:T(4,128)}, u32[]{:S(2)}) copy-start(f32[1,8,4,128]{1,2,3,0:T(4,128)} %copy.187) | copy-start | bytes 49156
  165.1 23.2 %copy-start.24 = (f32[2,8]{1,0:T(2,128)S(1)}, f32[2,8]{1,0:T(2,128)}, u32[]{:S(2)}) copy-start(f32[2,8]{1,0:T(2,128)} %param.22) | copy-start | bytes 196
  188.2 25.9 %slice-start = ((s8[8388608]{0:T(1024)(128)(4,1)}), s8[4194304]{0:T(1024)(128)(4,1)S(1)}, s32[]{:S(2)}) async-start(s8[8388608]{0:T(1024)(128)(4,1)} %bitcast.804), calls=%async_computation.4 | async-start | bytes 8388608
  239.3 54.8 %all-to-all-start = ((f32[2,512,512]{2,0,1:T(2,128)}), f32[2,512,512]{2,0,1:T(2,128)S(1)}, u32[]{:S(2)}, u32[]{:S(2)}) async-start(f32[2,512,512]{2,0,1:T(2,128)} %copy.132), calls=%async_computation | async-start | bytes 4194304 | tf_op jit(solution)/shard_map/all_to_all | solution.py:290
  360.7 52.1 %all-to-all-start.1 = ((f32[8,1,65536]{2,1,0:T(1,128)}), f32[8,1,65536]{2,1,0:T(1,128)S(1)}, u32[]{:S(2)}, u32[]{:S(2)}) async-start(f32[8,1,65536]{2,1,0:T(1,128)} %reshape.3793), calls=%async_computation.1 | async-start | bytes 4194304 | tf_op jit(solution)/shard_map/all_to_all | solution.py:301
  433.8 4.7 collective-permute-start.2
  435.1 3.8 collective-permute-start.3
  465.2 28.7 %copy-start.53 = (f32[8]{0:T(128)S(1)}, f32[8]{0:T(128)}, u32[]{:S(2)}) copy-start(f32[8]{0:T(128)} %get-tuple-element.981) | copy-start | bytes 100
  465.2 28.7 %copy-start.55 = (f32[8]{0:T(128)S(1)}, f32[8]{0:T(128)}, u32[]{:S(2)}) copy-start(f32[8]{0:T(128)} %get-tuple-element.985) | copy-start | bytes 100
  (48 other events, 594.3 us)
where the time goes:
time: 761 us; the launch traced here: 754 us
  matrix products  236 us (31%)
  blocking collectives  169 us (22%)
  other arithmetic  130 us (17%)
  local copies, waits for them, and re-layouts  101 us (13%)
  waiting for transfers between devices  96.2 us (13%)
  starting transfers between devices  19.4 us (3%)
    all_gather x12, blocking collectives, entering_2(): everything = jax.tree.map(lambda part: lax.all_gather(part, axis), value)  65.1 us
    all_to_all x1, blocking collectives, local(): lax.all_to_all(advance(pressure, operator_field, block_inverses, lower_sp...  52.3 us
    all_to_all x1, blocking collectives, local(): lax.all_to_all(coupled, 'az', split_axis=2, concat_axis=1, tiled=True)  51.9 us
    dot_general x10, matrix products, complex_einsum(): jnp.einsum(formula, left_im, right_re, precision=FULL_PRECISION)  48.1 us
    all_to_all x1, waiting for transfers between devices, local(): lax.all_to_all(coupled, 'az', split_axis=2, concat_axis=1, tiled=True)  48.1 us
    all_to_all x1, waiting for transfers between devices, local(): lax.all_to_all(advance(pressure, operator_field, block_inverses, lower_sp...  47.7 us
    unnamed x146, local copies, waits for them, and re-layouts  44 us
    dot_general x10, matrix products, complex_einsum(): jnp.einsum(formula, left_re, right_im, precision=FULL_PRECISION)  38.9 us
  transfers between devices with their start and end apart: 6, of which 3 were waited for; matrix products, arithmetic and copies ran while one was open for 3% of the time, Pallas kernels for 0%

commit v1 on v0

--- a/solution.py
+++ b/solution.py
@@ -8,6 +8,22 @@
 AZ_COLS = 128
 STEPS = 2
 FULL_PRECISION = lax.Precision.HIGHEST
+
+
+def pairwise_exchange(value, axis, split, join):
+    ways, here = (lax.axis_size(axis), lax.axis_index(axis))
+    width = value.shape[split] // ways
+    shape = list(value.shape)
+    shape[split] = width
+    height = shape[join]
+    shape[join] = height * ways
+    full = jnp.zeros(shape, value.dtype)
+    for mask in range(ways):
+        part = lax.dynamic_slice_in_dim(value, (here ^ mask) * width, width, axis=split)
+        if mask:
+            part = lax.ppermute(part, axis, [(d, d ^ mask) for d in range(ways)])
+        full = lax.dynamic_update_slice_in_dim(full, part, (here ^ mask) * height, axis=join)
+    return full
 
 
 def entering_2(value, axis, combine, identity, reverse):
@@ -297,9 +313,7 @@
             tiled=True,
         )
         coupled = couple_azimuths(columns, coupling_rows)
-        pressure = (
-            lax.all_to_all(coupled, "az", split_axis=2, concat_axis=1, tiled=True) * damp_rows[None]
-        )
+        pressure = pairwise_exchange(coupled, "az", 2, 1) * damp_rows[None]
     return pressure
 
 

time: 761 us -> 691 us (0.908)
  blocking collectives: 169 us -> 127 us
  local copies, waits for them, and re-layouts: 101 us -> 69.2 us
  other arithmetic: 130 us -> 100 us
  waiting for transfers between devices: 96.2 us -> 112 us
  starting transfers between devices: 19.4 us -> 34.6 us
    ppermute x0 -> x14, waiting for transfers between devices: none -> 61.6 us  [pairwise_exchange(): part = lax.ppermute(part, axis, [(d, d ^ mask) for d in range(ways)])]
    all_to_all x1 -> x0, blocking collectives: 51.9 us -> none  [local(): lax.all_to_all(coupled, 'az', split_axis=2, concat_axis=1, tiled=True)]
    all_to_all x1 -> x0, waiting for transfers between devices: 48.1 us -> none  [local(): lax.all_to_all(coupled, 'az', split_axis=2, concat_axis=1, tiled=True)]
    unnamed x146 -> x150, local copies, waits for them, and re-layouts: 44 us -> 21.1 us
    ppermute x0 -> x14, starting transfers between devices: none -> 20.9 us  [pairwise_exchange(): part = lax.ppermute(part, axis, [(d, d ^ mask) for d in range(ways)])]
    unnamed x15 -> x13, other arithmetic: 15.1 us -> 0.04 us
    all_to_all x2 -> x0, other arithmetic: 14.9 us -> none  [local(): lax.all_to_all(coupled, 'az', split_axis=2, concat_axis=1, tiled=True)]
    all_to_all x3 -> x0, local copies, waits for them, and re-layouts: 11 us -> none  [local(): lax.all_to_all(coupled, 'az', split_axis=2, concat_axis=1, tiled=True)]
  transfers between devices with their start and end apart: 6 -> 19, of which waited for: 3 -> 9; matrix products, arithmetic and copies ran while one was open for 3% -> 3% of each run, Pallas kernels for 0% -> 0%
where the time goes in v1:
time: 691 us; the launch traced here: 678 us
  matrix products  234 us (34%)
  blocking collectives  127 us (18%)
  waiting for transfers between devices  112 us (16%)
  other arithmetic  100 us (14%)
  local copies, waits for them, and re-layouts  69.2 us (10%)
  starting transfers between devices  34.6 us (5%)
    all_gather x12, blocking collectives, entering_2(): everything = jax.tree.map(lambda part: lax.all_gather(part, axis), value)  66.1 us
    ppermute x14, waiting for transfers between devices, pairwise_exchange(): part = lax.ppermute(part, axis, [(d, d ^ mask) for d in range(ways)])  61.6 us
    all_to_all x1, blocking collectives, local(): lax.all_to_all(advance(pressure, operator_field, block_inverses, lower_sp...  60.5 us
    all_to_all x1, waiting for transfers between devices, local(): lax.all_to_all(advance(pressure, operator_field, block_inverses, lower_sp...  47.4 us
    dot_general x10, matrix products, complex_einsum(): jnp.einsum(formula, left_im, right_re, precision=FULL_PRECISION)  42.7 us
    dot_general x10, matrix products, complex_einsum(): jnp.einsum(formula, left_im, right_im, precision=FULL_PRECISION)  37.2 us
    dot_general x10, matrix products, complex_einsum(): jnp.einsum(formula, left_re, right_im, precision=FULL_PRECISION)  36.6 us
    dot_general x10, matrix products, complex_einsum(): jnp.einsum(formula, left_re, right_re, precision=FULL_PRECISION)  35.6 us
  transfers between devices with their start and end apart: 19, of which 9 were waited for; matrix products, arithmetic and copies ran while one was open for 3% of the time, Pallas kernels for 0%

profile of v1, /device:TPU:0, one launch (start us, length us, event | category | flops | bytes accessed | tf_op | source)
XLA Modules:
  0.0 678.5 jit_solution(12606554541622081762)
XLA Ops:
  50.5 9.3 %fusion.46 = f32[4,512,8,128]{1,2,0,3:T(8,128)} fusion(f32[8,4,128,128]{3,2,1,0:T(8,128)S(1)} %copy-done.26, f32[4,128,512]{2,1,0:T(8,128)S(1)} %get-tuple-element.923), kind=kOutput, calls=%fused_computation.90 | convolution fusion | flops 3221225472 | bytes 11534336 | tf_op jit(solution)/shard_map/tbij,bjn->tbin/dot_general | solution.py:68
  67.0 7.4 %subtract_bitcast_fusion.1 = f32[8,4,128,512]{3,2,0,1:T(8,128)S(1)} fusion(f32[4,512,8,128]{1,3,2,0:T(8,128)S(1)} %fusion.38, f32[1,8,4,128,128]{4,3,2,1,0:T(8,128)S(1)} %copy-done.12, f32[4,128,512]{2,1,0:T(8,128)S(1)} %get-tuple-element.923), kind=kOutput, calls=%fused_computation.47 | convolution fusion | flops 3223322624 | bytes 19922944 | tf_op jit(solution)/shard_map/tbij,bjn->tbin/dot_general | solution.py:65
  74.6 12.7 %add_bitcast_fusion.1 = f32[8,4,128,512]{3,0,1,2:T(8,128)S(1)} fusion(f32[4,512,8,128]{1,2,0,3:T(8,128)} %fusion.46, f32[8,4,128,128]{3,2,1,0:T(8,128)S(1)} %copy-done.24, f32[4,128,512]{2,1,0:T(8,128)S(1)} %get-tuple-element.924), kind=kOutput, calls=%fused_computation.46 | convolution fusion | flops 3223322624 | bytes 19922944 | tf_op jit(solution)/shard_map/tbij,bjn->tbin/dot_general | solution.py:68
  104.7 7.5 %multiply_add_fusion = (f32[8,4,128,512]{3,0,1,2:T(8,128)}, f32[8,4,128,512]{3,0,1,2:T(8,128)}) fusion(f32[8,4,512]{2,0,1:T(8,128)S(1)} %pad_maximum_fusion.5, f32[8,4,128]{0,1,2:T(4,128)S(1)} %bitcast.808, f32[8,4,512]{2,0,1:T(8,128)S(1)} %pad_maximum_fusion.4, f32[8,4,128]{0,1,2:T(4,128)S(1)} %bitcast.804), kind=kLoop, calls=%fused_computation.44 | loop fusion | flops 12582912 | bytes 16941056 | tf_op jit(solution)/shard_map/add | solution.py:190
  112.1 15.0 %copy_subtract_fusion.2 = f32[8,4,128,512]{3,2,0,1:T(8,128)} fusion(f32[8,4,128,512]{3,2,0,1:T(8,128)} %copy-done.2, f32[8,4,128,512]{3,0,1,2:T(8,128)} %get-tuple-element.962), kind=kLoop, calls=%fused_computation.37 | loop fusion | flops 2097152 | bytes 25165824 | tf_op jit(solution)/shard_map/sub | solution.py:186
  128.3 18.7 %copy_subtract_fusion.1 = f32[8,4,128,512]{3,2,0,1:T(8,128)} fusion(f32[8,4,128,512]{3,0,1,2:T(8,128)} %get-tuple-element.961, f32[8,4,128,512]{3,0,1,2:T(8,128)} %copy-done.9), kind=kLoop, calls=%fused_computation.36 | loop fusion | flops 2097152 | bytes 25165824 | tf_op jit(solution)/shard_map/sub | solution.py:189
  166.3 23.4 %fusion.16 = (f32[8,4,128,512]{3,2,0,1:T(8,128)}, f32[8,4,128,512]{3,2,0,1:T(8,128)}) fusion(f32[8,4,128,512]{3,2,0,1:T(8,128)} %copy_subtract_fusion.1, f32[8,4,128,512]{3,0,1,2:T(8,128)} %get-tuple-element.973, f32[8,4,128]{2,0,1:T(8,128)S(1)} %copy.172, f32[8,4,512]{2,0,1:T(8,128)S(1)} %pad_maximum_fusion.7, f32[8,4,128,512]{3,2,0,1:T(8,128)} %copy_subtract_fusion.2, ...), kind=kLoop, calls=%fused_computation.33 | loop fusion | flops 12582912 | bytes 50429952 | tf_op jit(solution)/shard_map/sub | solution.py:211
  189.7 15.3 %fusion.28 = f32[1,4,128,512]{3,0,2,1:T(1,128)S(1)} fusion(f32[8,4,128,512]{3,2,0,1:T(8,128)} %get-tuple-element.971, f32[2,8]{1,0:T(2,128)S(1)} %copy-done.28), kind=kOutput, calls=%fused_computation.58 | convolution fusion | flops 25165824 | bytes 9437696 | tf_op jit(solution)/shard_map/t,tbin->bin/dot_general | solution.py:216
  205.0 15.5 %fusion.26 = f32[1,4,128,512]{3,0,2,1:T(1,128)S(1)} fusion(f32[8,4,128,512]{3,2,0,1:T(8,128)} %get-tuple-element.971, f32[2,8]{1,0:T(2,128)S(1)} %copy-done.28), kind=kOutput, calls=%fused_computation.56 | convolution fusion | flops 25165824 | bytes 9437696 | tf_op jit(solution)/shard_map/t,tbin->bin/dot_general | solution.py:217
  220.6 10.6 %fusion.32 = f32[1,4,128,512]{3,0,2,1:T(1,128)S(1)} fusion(f32[8,4,128,512]{3,2,0,1:T(8,128)S(1)} %bitcast.783, f32[2,8]{1,0:T(2,128)S(1)} %copy-done.28), kind=kOutput, calls=%fused_computation.62 | convolution fusion | flops 25165824 | bytes 9437696 | tf_op jit(solution)/shard_map/t,tbin->bin/dot_general | solution.py:214
  231.2 10.4 %fusion.30 = f32[1,4,128,512]{3,0,2,1:T(1,128)S(1)} fusion(f32[8,4,128,512]{3,2,0,1:T(8,128)S(1)} %bitcast.783, f32[2,8]{1,0:T(2,128)S(1)} %copy-done.28), kind=kOutput, calls=%fused_computation.60 | convolution fusion | flops 25165824 | bytes 9437696 | tf_op jit(solution)/shard_map/t,tbin->bin/dot_general | solution.py:219
  252.6 47.4 %all-to-all-done = f32[2,512,512]{2,0,1:T(2,128)S(1)} async-done(((f32[2,512,512]{2,0,1:T(2,128)}), f32[2,512,512]{2,0,1:T(2,128)S(1)}, u32[]{:S(2)}, u32[]{:S(2)}) %all-to-all-start) | async-done | bytes 2097184 | tf_op jit(solution)/shard_map/all_to_all | solution.py:306
  361.9 8.3 %collective-permute-done.3 = f32[2,64,512]{2,1,0:T(8,128)} collective-permute-done((f32[2,64,512]{2,1,0:T(8,128)}, f32[2,64,512]{2,1,0:T(8,128)}, u32[]{:S(2)}, u32[]{:S(2)}) %collective-permute-start.3) | collective-permute-done | bytes 262176 | tf_op jit(solution)/shard_map/ppermute | solution.py:24
  374.7 18.7 %collective-permute-done.6 = f32[2,64,512]{2,1,0:T(8,128)S(1)} collective-permute-done((f32[2,64,512]{2,1,0:T(8,128)S(1)}, f32[2,64,512]{2,1,0:T(8,128)S(1)}, u32[]{:S(2)}, u32[]{:S(2)}) %collective-permute-start.6) | collective-permute-done | bytes 262176 | tf_op jit(solution)/shard_map/ppermute | solution.py:24
  402.9 9.2 %fusion.44 = f32[4,512,8,128]{1,2,0,3:T(8,128)} fusion(f32[8,4,128,128]{3,2,1,0:T(8,128)S(1)} %copy-done.27, f32[4,128,512]{2,1,0:T(8,128)S(1)} %get-tuple-element.922), kind=kOutput, calls=%fused_computation.88 | convolution fusion | flops 3221225472 | bytes 11534336 | tf_op jit(solution)/shard_map/tbij,bjn->tbin/dot_general | solution.py:65
  412.1 7.7 %fusion.42 = f32[4,512,8,128]{1,2,0,3:T(8,128)S(1)} fusion(f32[8,4,128,128]{3,2,1,0:T(8,128)S(1)} %copy-done.27, f32[4,128,512]{2,1,0:T(8,128)S(1)} %get-tuple-element.921), kind=kOutput, calls=%fused_computation.86 | convolution fusion | flops 3221225472 | bytes 11534336 | tf_op jit(solution)/shard_map/tbij,bjn->tbin/dot_general | solution.py:68
  419.7 10.2 %subtract_bitcast_fusion = f32[8,4,128,512]{3,0,1,2:T(8,128)S(1)} fusion(f32[4,512,8,128]{1,2,0,3:T(8,128)} %fusion.44, f32[8,4,128,128]{3,2,1,0:T(8,128)S(1)} %copy-done.25, f32[4,128,512]{2,1,0:T(8,128)S(1)} %get-tuple-element.921), kind=kOutput, calls=%fused_computation.43 | convolution fusion | flops 3223322624 | bytes 19922944 | tf_op jit(solution)/shard_map/tbij,bjn->tbin/dot_general | solution.py:65
  430.1 7.7 %add_bitcast_fusion = f32[8,4,128,512]{3,0,1,2:T(8,128)S(1)} fusion(f32[4,512,8,128]{1,2,0,3:T(8,128)S(1)} %fusion.42, f32[8,4,128,128]{3,2,1,0:T(8,128)S(1)} %copy-done.25, f32[4,128,512]{2,1,0:T(8,128)S(1)} %get-tuple-element.922), kind=kOutput, calls=%fused_computation.42 | convolution fusion | flops 3223322624 | bytes 19922944 | tf_op jit(solution)/shard_map/tbij,bjn->tbin/dot_general | solution.py:68
  456.4 7.4 %add_subtract_fusion.1 = (f32[8,4,128,512]{3,0,1,2:T(8,128)S(1)}, f32[8,4,128,512]{3,0,1,2:T(8,128)S(1)}) fusion(f32[8,4,128,512]{3,0,1,2:T(8,128)} %copy-done.11, f32[8,4,512]{2,0,1:T(8,128)S(1)} %pad_maximum_fusion.9, f32[8,4,512]{2,0,1:T(8,128)S(1)} %pad_maximum_fusion.8, f32[8,4,128]{0,1,2:T(4,128)} %bitcast.807, f32[8,4,128]{0,1,2:T(4,128)S(1)} %bitcast.805, ...), kind=kLoop, calls=%fused_computation.40 | loop fusion | flops 16777216 | bytes 33718272 | tf_op jit(solution)/shard_map/sub | solution.py:189
  498.2 7.3 %fusion.18 = f32[1,4,128,512]{3,0,2,1:T(1,128)S(1)} fusion(f32[8,4,128,512]{3,0,1,2:T(8,128)S(1)} %get-tuple-element.957, f32[2,8]{1,0:T(2,128)S(1)} %copy-done.28), kind=kOutput, calls=%fused_computation.48 | convolution fusion | flops 25165824 | bytes 9437696 | tf_op jit(solution)/shard_map/t,tbin->bin/dot_general | solution.py:217
  505.6 7.6 %fusion.24 = f32[1,4,128,512]{3,0,2,1:T(1,128)S(1)} fusion(f32[8,4,128,512]{3,0,1,2:T(8,128)S(1)} %get-tuple-element.958, f32[2,8]{1,0:T(2,128)S(1)} %copy-done.28), kind=kOutput, calls=%fused_computation.54 | convolution fusion | flops 25165824 | bytes 9437696 | tf_op jit(solution)/shard_map/t,tbin->bin/dot_general | solution.py:214
  524.2 60.5 %all_to_all.30 = f32[2,512,512]{2,0,1:T(2,128)S(1)} all-to-all(f32[2,512,512]{2,0,1:T(2,128)S(1)} %copy.128), channel_id=1, replica_groups=mesh['depth'=4,'az'=8] {'az'}, dimensions={1} | all-to-all | bytes 4194304 | tf_op jit(solution)/shard_map/all_to_all | solution.py:306
  643.1 10.4 %collective-permute-done.12 = f32[2,64,512]{2,1,0:T(8,128)S(1)} collective-permute-done((f32[2,64,512]{2,1,0:T(8,128)S(1)}, f32[2,64,512]{2,1,0:T(8,128)S(1)}, u32[]{:S(2)}, u32[]{:S(2)}) %collective-permute-start.12) | collective-permute-done | bytes 262176 | tf_op jit(solution)/shard_map/ppermute | solution.py:24
  656.8 19.6 %collective-permute-done.15 = f32[2,64,512]{2,1,0:T(8,128)S(1)} collective-permute-done((f32[2,64,512]{2,1,0:T(8,128)S(1)}, f32[2,64,512]{2,1,0:T(8,128)S(1)}, u32[]{:S(2)}, u32[]{:S(2)}) %collective-permute-start.15) | collective-permute-done | bytes 262176 | tf_op jit(solution)/shard_map/ppermute | solution.py:24
  (391 shorter events, 315.6 us)
Async XLA Ops:
  0.0 351.5 %copy-start = (f32[5,6]{1,0:T(8,128)S(1)}, f32[5,6]{1,0:T(8,128)}, u32[]{:S(2)}) copy-start(f32[5,6]{1,0:T(8,128)} %param.26) | copy-start | bytes 364
  1.4 45.1 %collective-permute-start = (f32[2,1,512]{2,1,0:T(1,128)}, f32[2,1,512]{2,1,0:T(1,128)}, u32[]{:S(2)}, u32[]{:S(2)}) collective-permute-start(f32[2,1,512]{2,1,0:T(1,128)} %get-tuple-element.955), channel_id=1, source_target_pairs={{8,0},{16,8},{24,16},{9,1},{17,9},{25,17},{10,2},{18,10},{26,18},{... | collective-permute-start | bytes 12296 | tf_op jit(solution)/shard_map/ppermute | solution.py:57
  2.7 43.8 %collective-permute-start.1 = (f32[2,1,512]{2,1,0:T(1,128)}, f32[2,1,512]{2,1,0:T(1,128)}, u32[]{:S(2)}, u32[]{:S(2)}) collective-permute-start(f32[2,1,512]{2,1,0:T(1,128)} %get-tuple-element.956), channel_id=1, source_target_pairs={{0,8},{8,16},{16,24},{1,9},{9,17},{17,25},{2,10},{10,18},{18,26},{... | collective-permute-start | bytes 12296 | tf_op jit(solution)/shard_map/ppermute | solution.py:55
  13.8 32.7 %copy-start.5 = (f32[2,512,512]{2,1,0:T(8,128)S(1)}, f32[2,512,512]{2,1,0:T(8,128)}, u32[]{:S(2)}) copy-start(f32[2,512,512]{2,1,0:T(8,128)} %param.18) | copy-start | bytes 6291460
  128.3 31.1 %copy-start.54 = (f32[8]{0:T(128)S(1)}, f32[8]{0:T(128)}, u32[]{:S(2)}) copy-start(f32[8]{0:T(128)} %get-tuple-element.989) | copy-start | bytes 100
  128.3 31.0 %copy-start.55 = (f32[8]{0:T(128)S(1)}, f32[8]{0:T(128)}, u32[]{:S(2)}) copy-start(f32[8]{0:T(128)} %get-tuple-element.993) | copy-start | bytes 100
  245.5 54.5 %all-to-all-start = ((f32[2,512,512]{2,0,1:T(2,128)}), f32[2,512,512]{2,0,1:T(2,128)S(1)}, u32[]{:S(2)}, u32[]{:S(2)}) async-start(f32[2,512,512]{2,0,1:T(2,128)} %copy.122), calls=%async_computation | async-start | bytes 4194304 | tf_op jit(solution)/shard_map/all_to_all | solution.py:306
  350.1 7.8 %collective-permute-start.2 = (f32[2,64,512]{2,1,0:T(8,128)}, f32[2,64,512]{2,1,0:T(8,128)}, u32[]{:S(2)}, u32[]{:S(2)}) collective-permute-start(f32[2,64,512]{2,1,0:T(8,128)} %get-tuple-element.947), channel_id=1, source_target_pairs={{0,1},{1,0},{2,3},{3,2},{4,5},{5,4},{6,7},{7,6},{8,9},{9,8},{10,11... | collective-permute-start | bytes 786440 | tf_op jit(solution)/shard_map/ppermute | solution.py:24
  351.7 18.5 %collective-permute-start.3 = (f32[2,64,512]{2,1,0:T(8,128)}, f32[2,64,512]{2,1,0:T(8,128)}, u32[]{:S(2)}, u32[]{:S(2)}) collective-permute-start(f32[2,64,512]{2,1,0:T(8,128)} %get-tuple-element.946), channel_id=1, source_target_pairs={{0,2},{1,3},{2,0},{3,1},{4,6},{5,7},{6,4},{7,5},{8,10},{9,11},{10,... | collective-permute-start | bytes 786440 | tf_op jit(solution)/shard_map/ppermute | solution.py:24
  351.7 22.0 %collective-permute-start.4 = (f32[2,64,512]{2,1,0:T(8,128)}, f32[2,64,512]{2,1,0:T(8,128)}, u32[]{:S(2)}, u32[]{:S(2)}) collective-permute-start(f32[2,64,512]{2,1,0:T(8,128)} %get-tuple-element.945), channel_id=1, source_target_pairs={{0,3},{1,2},{2,1},{3,0},{4,7},{5,6},{6,5},{7,4},{8,11},{9,10},{10,... | collective-permute-start | bytes 786440 | tf_op jit(solution)/shard_map/ppermute | solution.py:24
  354.0 20.7 %collective-permute-start.5 = (f32[2,64,512]{2,1,0:T(8,128)}, f32[2,64,512]{2,1,0:T(8,128)S(1)}, u32[]{:S(2)}, u32[]{:S(2)}) collective-permute-start(f32[2,64,512]{2,1,0:T(8,128)} %get-tuple-element.944), channel_id=1, source_target_pairs={{0,4},{1,5},{2,6},{3,7},{4,0},{5,1},{6,2},{7,3},{8,12},{9,13},{10,... | collective-permute-start | bytes 786440 | tf_op jit(solution)/shard_map/ppermute | solution.py:24
  354.9 38.5 %collective-permute-start.6 = (f32[2,64,512]{2,1,0:T(8,128)S(1)}, f32[2,64,512]{2,1,0:T(8,128)S(1)}, u32[]{:S(2)}, u32[]{:S(2)}) collective-permute-start(f32[2,64,512]{2,1,0:T(8,128)S(1)} %get-tuple-element.943), channel_id=1, source_target_pairs={{0,5},{1,4},{2,7},{3,6},{4,1},{5,0},{6,3},{7,2},{8,13},{9,12},{10,... | collective-permute-start | bytes 786440 | tf_op jit(solution)/shard_map/ppermute | solution.py:24
  357.9 35.5 %collective-permute-start.7 = (f32[2,64,512]{2,1,0:T(8,128)S(1)}, f32[2,64,512]{2,1,0:T(8,128)S(1)}, u32[]{:S(2)}, u32[]{:S(2)}) collective-permute-start(f32[2,64,512]{2,1,0:T(8,128)S(1)} %get-tuple-element.942), channel_id=1, source_target_pairs={{0,6},{1,7},{2,4},{3,5},{4,2},{5,3},{6,0},{7,1},{8,14},{9,15},{10,... | collective-permute-start | bytes 786440 | tf_op jit(solution)/shard_map/ppermute | solution.py:24
  370.2 23.3 %collective-permute-start.8 = (f32[2,64,512]{2,1,0:T(8,128)S(1)}, f32[2,64,512]{2,1,0:T(8,128)S(1)}, u32[]{:S(2)}, u32[]{:S(2)}) collective-permute-start(f32[2,64,512]{2,1,0:T(8,128)S(1)} %get-tuple-element.941), channel_id=1, source_target_pairs={{0,7},{1,6},{2,5},{3,4},{4,3},{5,2},{6,1},{7,0},{8,15},{9,14},{10,... | collective-permute-start | bytes 786440 | tf_op jit(solution)/shard_map/ppermute | solution.py:24
  394.6 2.8 collective-permute-start.10
  395.9 4.2 collective-permute-start.9
  633.7 42.8 %copy-start.8 = (f32[4,128,512]{2,1,0:T(8,128)S(1)}, f32[4,128,512]{2,1,0:T(8,128)}, u32[]{:S(2)}) copy-start(f32[4,128,512]{2,1,0:T(8,128)} %copy-done.6) | copy-start | bytes 3145732
  633.7 7.5 %collective-permute-start.11 = (f32[2,64,512]{2,1,0:T(8,128)S(1)}, f32[2,64,512]{2,1,0:T(8,128)S(1)}, u32[]{:S(2)}, u32[]{:S(2)}) collective-permute-start(f32[2,64,512]{2,1,0:T(8,128)S(1)} %get-tuple-element.931), channel_id=1, source_target_pairs={{0,1},{1,0},{2,3},{3,2},{4,5},{5,4},{6,7},{7,6},{8,9},{9,8},{10,11... | collective-permute-start | bytes 786440 | tf_op jit(solution)/shard_map/ppermute | solution.py:24
  635.2 18.2 %collective-permute-start.12 = (f32[2,64,512]{2,1,0:T(8,128)S(1)}, f32[2,64,512]{2,1,0:T(8,128)S(1)}, u32[]{:S(2)}, u32[]{:S(2)}) collective-permute-start(f32[2,64,512]{2,1,0:T(8,128)S(1)} %get-tuple-element.930), channel_id=1, source_target_pairs={{0,2},{1,3},{2,0},{3,1},{4,6},{5,7},{6,4},{7,5},{8,10},{9,11},{10,... | collective-permute-start | bytes 786440 | tf_op jit(solution)/shard_map/ppermute | solution.py:24
  635.2 21.5 %collective-permute-start.13 = (f32[2,64,512]{2,1,0:T(8,128)S(1)}, f32[2,64,512]{2,1,0:T(8,128)S(1)}, u32[]{:S(2)}, u32[]{:S(2)}) collective-permute-start(f32[2,64,512]{2,1,0:T(8,128)S(1)} %get-tuple-element.929), channel_id=1, source_target_pairs={{0,3},{1,2},{2,1},{3,0},{4,7},{5,6},{6,5},{7,4},{8,11},{9,10},{10,... | collective-permute-start | bytes 786440 | tf_op jit(solution)/shard_map/ppermute | solution.py:24
  637.3 19.5 %collective-permute-start.14 = (f32[2,64,512]{2,1,0:T(8,128)S(1)}, f32[2,64,512]{2,1,0:T(8,128)S(1)}, u32[]{:S(2)}, u32[]{:S(2)}) collective-permute-start(f32[2,64,512]{2,1,0:T(8,128)S(1)} %get-tuple-element.928), channel_id=1, source_target_pairs={{0,4},{1,5},{2,6},{3,7},{4,0},{5,1},{6,2},{7,3},{8,12},{9,13},{10,... | collective-permute-start | bytes 786440 | tf_op jit(solution)/shard_map/ppermute | solution.py:24
  638.2 38.2 %collective-permute-start.15 = (f32[2,64,512]{2,1,0:T(8,128)S(1)}, f32[2,64,512]{2,1,0:T(8,128)S(1)}, u32[]{:S(2)}, u32[]{:S(2)}) collective-permute-start(f32[2,64,512]{2,1,0:T(8,128)S(1)} %get-tuple-element.927), channel_id=1, source_target_pairs={{0,5},{1,4},{2,7},{3,6},{4,1},{5,0},{6,3},{7,2},{8,13},{9,12},{10,... | collective-permute-start | bytes 786440 | tf_op jit(solution)/shard_map/ppermute | solution.py:24
  641.2 35.2 %collective-permute-start.16 = (f32[2,64,512]{2,1,0:T(8,128)S(1)}, f32[2,64,512]{2,1,0:T(8,128)S(1)}, u32[]{:S(2)}, u32[]{:S(2)}) collective-permute-start(f32[2,64,512]{2,1,0:T(8,128)S(1)} %get-tuple-element.926), channel_id=1, source_target_pairs={{0,6},{1,7},{2,4},{3,5},{4,2},{5,3},{6,0},{7,1},{8,14},{9,15},{10,... | collective-permute-start | bytes 786440 | tf_op jit(solution)/shard_map/ppermute | solution.py:24
  653.5 23.0 %collective-permute-start.17 = (f32[2,64,512]{2,1,0:T(8,128)S(1)}, f32[2,64,512]{2,1,0:T(8,128)S(1)}, u32[]{:S(2)}, u32[]{:S(2)}) collective-permute-start(f32[2,64,512]{2,1,0:T(8,128)S(1)} %get-tuple-element.925), channel_id=1, source_target_pairs={{0,7},{1,6},{2,5},{3,4},{4,3},{5,2},{6,1},{7,0},{8,15},{9,14},{10,... | collective-permute-start | bytes 786440 | tf_op jit(solution)/shard_map/ppermute | solution.py:24
  (65 other events, 771.3 us)
